TPU v7x, 128 devices: a whole 4x4x4 slice. The times are simulated.
128 devices in a mesh: pair: 8 (over y_hi, x), mode: 16 (over y_lo, z, core).
Axes of the slice: x: 4, y: 4 (y_hi: 2, y_lo: 2; y = y_hi * 2 + y_lo), z: 4, core: 2. Of those that a mesh axis runs over, the one named last changes fastest.
Arguments:
- time_pairs: int32 [8, 2], P('pair'), may hold values from 0 to 7, as said below
- slot_of: int32 [8], replicated, may hold values from 0 to 7, each once
- elementals: bfloat16 [8, 4, 2, 1536, 1536], P('pair', None, None, 'mode'), may hold values from -0.109375 to 0.109375
- propagators: bfloat16 [8, 2, 1536, 1536], P('pair', None, 'mode'), may hold values from -6 to 6
Outputs:
- correlation: float32 [8, 4, 4, 2], P('pair')
- sink_block: bfloat16 [8, 4, 2, 1536, 1536], P('pair', None, None, 'mode')
Inputs may be any that keep to these rules, and one draw needn't show every extreme that they name: `time_pairs`: the first column names each of the 8 timeslices once; in every row the second column differs from the first. `slot_of`: names every slot once; slot k of elementals lies on pair index k.
All inputs are finite; a program needn't handle non-finite values.
Results may differ from a plain program's by a relative error of at most 0.0051.
Values may be sent and summed in bfloat16 or wider, within the bound.
A program may use at most 128 MiB of HBM per device.

v0:
```python
import jax
import jax.numpy as jnp
from jax import lax
from jax.sharding import PartitionSpec as P


def body(time_pairs, slot_of, elementals, propagators):
    pair_count = time_pairs.shape[0]
    op_count = elementals.shape[1]
    row_count = elementals.shape[3]
    order_size = elementals.shape[4]
    slot_count = slot_of.shape[0]
    positions = jnp.arange(slot_count, dtype=jnp.int32)
    flat_times = time_pairs.reshape(-1)
    wanted = jnp.sum(
        jnp.where(flat_times[:, None] == positions[None, :], slot_of[None, :], 0), axis=1
    )
    slab_size = op_count * 2 * row_count * order_size
    empty_slabs = jnp.zeros((wanted.shape[0], slab_size), jnp.bfloat16)
    segment = lax.all_gather(elementals, "pair", axis=0, tiled=True)
    count = segment.shape[0]
    indices = jnp.arange(count, dtype=jnp.int32)
    match = wanted[:, None] == indices[None, :]
    picked = jnp.dot(
        match.astype(jnp.bfloat16),
        segment.reshape(count, slab_size),
        preferred_element_type=jnp.float32,
    ).astype(jnp.bfloat16)
    found = jnp.any(match, axis=1)
    chosen = jnp.where(found[:, None], picked, empty_slabs)
    chosen = chosen.reshape(pair_count, 2, op_count, 2, row_count, order_size)
    sink_ops = chosen[0, 0]
    source_ops = chosen[0, 1]
    propagator = propagators[0]
    segment = lax.all_gather(propagator, "mode", axis=1, tiled=True)
    real_part = jnp.einsum(
        "grk,kn->grn", sink_ops[:, 0], segment[0], preferred_element_type=jnp.float32
    ) - jnp.einsum("grk,kn->grn", sink_ops[:, 1], segment[1], preferred_element_type=jnp.float32)
    imag_part = jnp.einsum(
        "grk,kn->grn", sink_ops[:, 0], segment[1], preferred_element_type=jnp.float32
    ) + jnp.einsum("grk,kn->grn", sink_ops[:, 1], segment[0], preferred_element_type=jnp.float32)
    summed = jnp.stack([real_part, imag_part], 1)
    real_part = jnp.einsum(
        "gjk,ik->gji", source_ops[:, 0], segment[0], preferred_element_type=jnp.float32
    ) + jnp.einsum("gjk,ik->gji", source_ops[:, 1], segment[1], preferred_element_type=jnp.float32)
    imag_part = jnp.einsum(
        "gjk,ik->gji", source_ops[:, 1], segment[0], preferred_element_type=jnp.float32
    ) - jnp.einsum("gjk,ik->gji", source_ops[:, 0], segment[1], preferred_element_type=jnp.float32)
    placed = jnp.stack([real_part, imag_part], 1)
    block = summed.astype(jnp.bfloat16)
    block_list = [block]
    turned = placed.astype(jnp.bfloat16)
    received = lax.all_to_all(turned, "mode", split_axis=3, concat_axis=2, tiled=True)
    real_part = jnp.einsum(
        "gij,hji->gh", block[:, 0], received[:, 0], preferred_element_type=jnp.float32
    ) - jnp.einsum("gij,hji->gh", block[:, 1], received[:, 1], preferred_element_type=jnp.float32)
    imag_part = jnp.einsum(
        "gij,hji->gh", block[:, 0], received[:, 1], preferred_element_type=jnp.float32
    ) + jnp.einsum("gij,hji->gh", block[:, 1], received[:, 0], preferred_element_type=jnp.float32)
    partial_list = [jnp.stack([real_part, imag_part], -1)]
    partials = jnp.stack(partial_list)
    totals = lax.psum(partials, "mode")
    correlation = totals / order_size
    return (correlation, jnp.stack(block_list))


def solution(mesh):
    in_specs = (
        P("pair", None),
        P(),
        P("pair", None, None, "mode", None),
        P("pair", None, "mode", None),
    )
    out_specs = (P("pair", None, None, None), P("pair", None, None, "mode", None))
    return jax.shard_map(body, mesh=mesh, in_specs=in_specs, out_specs=out_specs, check_vma=False)
```

profile of v0, /device:TPU:1, one launch (start us, length us, event | category | flops | bytes accessed | tf_op | source)
XLA Modules:
  0.0 395.0 jit_solution(379946908830714107)
XLA Ops:
  9.1 209.3 %all-gather.4.cloned.1.call-done = bf16[8,4,2,96,1536]{4,3,2,1,0:T(8,128)(2,1)} async-done(((bf16[1,4,2,96,1536]{4,3,2,1,0:T(8,128)(2,1)}), bf16[8,4,2,96,1536]{4,3,2,1,0:T(8,128)(2,1)}) %all-gather.4.cloned.1.call-update) | async-done | bytes 18874384 | tf_op jit(solution)/shard_map/all_gather | solution.py:20
  218.4 20.8 %copy.37 = bf16[1,8,768,1536]{3,1,2,0:T(8,128)(2,1)} copy(bf16[1,8,768,1536]{3,2,1,0:T(8,128)(2,1)} %bitcast.110) | data formatting | bytes 37748736
  239.2 9.7 %fusion = bf16[2,1179648]{1,0:T(2,128)(2,1)S(1)} fusion(bf16[8,1179648]{1,0:T(8,128)(2,1)} %bitcast.111, pred[2]{0:T(512)(128)(4,1)S(1)} %fusion.28, s32[2]{0:T(128)S(1)} %fusion.27), kind=kOutput, calls=%fused_computation.1 | convolution fusion | flops 42467344 | bytes 23592970 | tf_op jit(solution)/shard_map/dot_general | solution.py:24
  249.9 1.7 copy.52
  251.8 24.1 %all-gather.6.cloned.1.call-done = bf16[1,2,1536,1536]{3,2,1,0:T(8,128)(2,1)} async-done(((bf16[1,2,96,1536]{3,2,1,0:T(8,128)(2,1)}), bf16[1,2,1536,1536]{3,2,1,0:T(8,128)(2,1)}) %all-gather.6.cloned.1.call-update) | async-done | bytes 9437200 | tf_op jit(solution)/shard_map/all_gather | solution.py:35
  275.9 4.5 %fusion.2 = f32[4,96,1536]{2,1,0:T(8,128)S(1)} fusion(bf16[1,2,1536,1536]{3,2,1,0:T(8,128)(2,1)} %all-gather.6.cloned.1.call-done, bf16[4,2,96,1536]{3,2,0,1:T(8,128)(2,1)S(1)} %bitcast.120), kind=kOutput, calls=%fused_computation.6 | convolution fusion | flops 1811939328 | bytes 8257536 | tf_op jit(solution)/shard_map/gjk,ik->gji/dot_general | solution.py:46
  281.0 2.0 fusion.3
  283.0 2.0 fusion.18
  285.1 2.0 fusion.17
  287.3 3.7 copy.27
  291.0 5.2 %all-to-all-start = ((bf16[4,2,96,1536]{2,0,1,3:T(4,128)(2,1)}), bf16[4,2,96,1536]{2,0,1,3:T(4,128)(2,1)S(1)}, u32[]{:S(2)}, u32[]{:S(2)}) async-start(bf16[4,2,96,1536]{2,0,1,3:T(4,128)(2,1)} %copy.27), calls=%async_computation | async-start | bytes 6291456 | tf_op jit(solution)/shard_map/all_to_all | solution.py:53
  296.3 4.8 %fusion.1 = f32[4,96,1536]{2,1,0:T(8,128)S(1)} fusion(bf16[1,2,1536,1536]{3,2,1,0:T(8,128)(2,1)} %all-gather.6.cloned.1.call-done, bf16[4,2,96,1536]{3,2,0,1:T(8,128)(2,1)} %bitcast.116), kind=kOutput, calls=%fused_computation.5 | convolution fusion | flops 1811939328 | bytes 8257536 | tf_op jit(solution)/shard_map/grk,kn->grn/dot_general | solution.py:41
  301.2 4.4 %fusion.4 = f32[4,96,1536]{2,1,0:T(8,128)S(1)} fusion(bf16[1,2,1536,1536]{3,2,1,0:T(8,128)(2,1)} %all-gather.6.cloned.1.call-done, bf16[4,2,96,1536]{3,2,0,1:T(8,128)(2,1)S(1)} %bitcast.117), kind=kOutput, calls=%fused_computation.8 | convolution fusion | flops 1811939328 | bytes 8257536 | tf_op jit(solution)/shard_map/grk,kn->grn/dot_general | solution.py:36
  305.6 2.0 fusion.13
  307.6 2.0 fusion.16
  310.7 1.6 copy.34
  312.2 24.4 %all-to-all-done = bf16[4,2,96,1536]{2,0,1,3:T(4,128)(2,1)S(1)} async-done(((bf16[4,2,96,1536]{2,0,1,3:T(4,128)(2,1)}), bf16[4,2,96,1536]{2,0,1,3:T(4,128)(2,1)S(1)}, u32[]{:S(2)}, u32[]{:S(2)}) %all-to-all-start) | async-done | bytes 2359328 | tf_op jit(solution)/shard_map/all_to_all | solution.py:53
  336.6 5.3 %copy.50 = bf16[4,2,96,16,96]{2,3,0,4,1:T(8,128)(2,1)} copy(bf16[4,2,96,16,96]{2,0,1,4,3:T(4,128)(2,1)S(1)} %bitcast.113) | data formatting | bytes 4718592 | tf_op jit(solution)/shard_map/all_to_all | solution.py:53
  341.9 6.4 %all_to_all.16 = bf16[4,2,1536,96]{2,0,3,1:T(4,128)(2,1)S(1)} reshape(bf16[4,2,16,96,96]{3,2,0,4,1:T(8,128)(2,1)} %bitcast.114) | data formatting | bytes 4718592 | tf_op jit(solution)/shard_map/all_to_all | solution.py:53
  348.3 2.0 convolution_bitcast_fusion
  350.4 2.0 convolution_bitcast_fusion.2
  352.4 2.1 fusion.20
  354.5 1.5 fusion.22
  356.0 31.6 %psum.7 = f32[1,4,4,2]{2,1,3,0:T(4,128)S(1)} all-reduce(f32[1,4,4,2]{2,1,3,0:T(4,128)S(1)} %maximum_bitcast_fusion), channel_id=1, replica_groups=mesh['pair'=8,'mode'=16] {'mode'}, use_global_device_ids=true, to_apply=%region_2.3 | all-reduce | flops 32 | bytes 256 | tf_op jit(solution)/shard_map/psum | solution.py:62
  (37 shorter events, 5.6 us)
Async XLA Ops:
  7.2 1.5 copy-start.6
  7.2 1.5 copy-start.7
  7.2 211.2 %all-gather.4.cloned.1.call-start = ((), (), s32[]{:S(2)}) async-start(), calls=%async_computation.1 | async-start | bytes 21233664 | tf_op jit(solution)/shard_map/all_gather | solution.py:20
  7.9 268.0 %all-gather.6.cloned.1.call-start = ((), (), s32[]{:S(2)}) async-start(), calls=%async_computation.2 | async-start | bytes 10027008 | tf_op jit(solution)/shard_map/all_gather | solution.py:35
  275.9 5.1 %copy-start.5 = (bf16[1,2,1536,1536]{3,2,1,0:T(8,128)(2,1)S(1)}, bf16[1,2,1536,1536]{3,2,1,0:T(8,128)(2,1)}, u32[]{:S(2)}) copy-start(bf16[1,2,1536,1536]{3,2,1,0:T(8,128)(2,1)} %all-gather.6.cloned.1.call-done) | copy-start | bytes 28311556
  291.0 45.6 %all-to-all-start = ((bf16[4,2,96,1536]{2,0,1,3:T(4,128)(2,1)}), bf16[4,2,96,1536]{2,0,1,3:T(4,128)(2,1)S(1)}, u32[]{:S(2)}, u32[]{:S(2)}) async-start(bf16[4,2,96,1536]{2,0,1,3:T(4,128)(2,1)} %copy.27), calls=%async_computation | async-start | bytes 6291456 | tf_op jit(solution)/shard_map/all_to_all | solution.py:53
  296.3 4.9 %copy-start = (bf16[1,1,4,2,96,1536]{5,4,2,3,1,0:T(8,128)(2,1)S(1)}, bf16[1,1,4,2,96,1536]{5,4,2,3,1,0:T(8,128)(2,1)}, u32[]{:S(2)}) copy-start(bf16[1,1,4,2,96,1536]{5,4,2,3,1,0:T(8,128)(2,1)} %copy.52) | copy-start | bytes 7077892
  296.3 9.3 %slice-start = ((s8[9437184]{0:T(1024)(128)(4,1)}), s8[4194304]{0:T(1024)(128)(4,1)S(1)}, s32[]{:S(2)}) async-start(s8[9437184]{0:T(1024)(128)(4,1)} %bitcast.126), calls=%async_computation.3 | async-start | bytes 8388608
  296.3 9.3 %slice-start.1 = ((s8[9437184]{0:T(1024)(128)(4,1)}), s8[4194304]{0:T(1024)(128)(4,1)S(1)}, s32[]{:S(2)}) async-start(s8[9437184]{0:T(1024)(128)(4,1)} %bitcast.126), calls=%async_computation.4 | async-start | bytes 8388608
  301.1 4.4 %slice-start.2 = ((s8[9437184]{0:T(1024)(128)(4,1)}), s8[1048576]{0:T(1024)(128)(4,1)S(1)}, s32[]{:S(2)}) async-start(s8[9437184]{0:T(1024)(128)(4,1)} %bitcast.126), calls=%async_computation.5 | async-start | bytes 2097152
  307.6 2.0 copy-start.3
  309.6 1.0 copy-start.1
  341.9 6.4 %copy-start.4 = (bf16[4,96,1536]{2,1,0:T(8,128)(2,1)S(1)}, bf16[4,96,1536]{2,1,0:T(8,128)(2,1)}, u32[]{:S(2)}) copy-start(bf16[4,96,1536]{2,1,0:T(8,128)(2,1)} %copy-done.3) | copy-start | bytes 3538948
  350.4 2.0 copy-start.2
Sparse Core Ops, SparseCore 0:
  10.4 207.9 all-gather.3
  220.0 55.8 all-gather.5
where the time goes:
time: 398 us; the launch traced here: 395 us
  waiting for transfers between devices  259 us (65%)
  local copies, waits for them, and re-layouts  42.7 us (11%)
  matrix products  41.1 us (10%)
  blocking collectives  31.6 us (8%)
  between operations  14.3 us (4%)
  starting transfers between devices  5.32 us (1%)
    all_gather x1, waiting for transfers between devices, body(): segment = lax.all_gather(elementals, 'pair', axis=0, tiled=True)  209 us
    psum x1, blocking collectives, body(): totals = lax.psum(partials, 'mode')  31.6 us
    unnamed x28, local copies, waits for them, and re-layouts  27 us
    all_to_all x1, waiting for transfers between devices, body(): lax.all_to_all(turned, 'mode', split_axis=3, concat_axis=2, tiled=True)  24.4 us
    all_gather x1, waiting for transfers between devices, body(): segment = lax.all_gather(propagator, 'mode', axis=1, tiled=True)  24.1 us
    all_to_all x2, local copies, waits for them, and re-layouts, body(): lax.all_to_all(turned, 'mode', split_axis=3, concat_axis=2, tiled=True)  11.7 us
    dot_general x1, matrix products, body(): jnp.dot(match.astype(jnp.bfloat16), segment.reshape(count, slab_size), pr...  9.68 us
  transfers between devices with their start and end apart: 3, of which 3 were waited for; matrix products, arithmetic and copies ran while one was open for 12% of the time, Pallas kernels for 0%

commit v1 on v0

v1 whole, which is shorter than its diff:
```python
import jax
import jax.numpy as jnp
from jax import lax
from jax.experimental import pallas as pl
from jax.experimental.pallas import tpu as pltpu
from jax.sharding import PartitionSpec as P

MESH = pl.DeviceIdType.MESH
F32 = jnp.float32
BF16 = jnp.bfloat16
XS = 4
MODES = 16
OPS = 4
SLOTS = 8


def kernel(want_ref, elem, prop, sink_hbm, corr_ref,
           r0, r1, r2, r3, staged, w_sink, w_source, tau, stack, stack2, turned, arrived, sink,
           want_all, want_smem, parts,
           want_send, want_recv, p1_send, p1_recv, y_send, y_recv, p2_send, p2_recv,
           tau_send, tau_recv, t_send, t_recv, ps_send, ps_recv, local, out_sem):
    rows = elem.shape[2]
    order = elem.shape[3]
    quarter = order // XS
    gathered = (r0, r1, r2, r3)

    pair = lax.axis_index("pair")
    mode = lax.axis_index("mode")
    yh, x = pair // XS, pair % XS
    yl, z, core = mode // 8, (mode // 2) % 4, mode % 2

    def at_x(step):
        return (yh * XS + (x + step) % XS, mode)

    y_partner = ((1 - yh) * XS + x, mode)

    def chunk(y_at, z_at, core_at):
        return y_at * 8 + z_at * 2 + core_at

    def at_mode(y_at, z_at, core_at):
        return (pair, chunk(y_at, z_at, core_at))

    def remote(src, dst, send, recv, device):
        return pltpu.make_async_remote_copy(
            src_ref=src, dst_ref=dst, send_sem=send, recv_sem=recv,
            device_id=device, device_id_type=MESH)

    barrier = pltpu.get_barrier_semaphore()
    for step in range(1, XS):
        pl.semaphore_signal(barrier, inc=1, device_id=at_x(step), device_id_type=MESH)
    pl.semaphore_signal(barrier, inc=1, device_id=y_partner, device_id_type=MESH)

    @pl.loop(1, MODES)
    def _(step):
        pl.semaphore_signal(barrier, inc=1, device_id=(pair, (mode + step) % MODES), device_id_type=MESH)

    pl.semaphore_wait(barrier, XS - 1 + 1 + MODES - 1)

    want_copies = [
        remote(want_ref, want_all.at[x], want_send.at[s - 1], want_recv.at[s - 1], at_x(s))
        for s in range(1, XS)
    ]
    for copy in want_copies:
        copy.start()
    own_want = pltpu.make_async_copy(want_ref, want_all.at[x], local.at[0])
    own_want.start()

    def columns(at):
        return pl.ds(pl.multiple_of(at * quarter, 128), quarter)

    def stage1(o):
        copies = []
        for s in (2, 1, 3):
            copies.append(remote(
                elem.at[o, :, :, columns((x + s) % XS)], gathered[o].at[pair],
                p1_send.at[o, s - 1], p1_recv.at[o, s - 1], at_x(s)))
        own = pltpu.make_async_copy(elem.at[o, :, :, columns(x)], gathered[o].at[pair], local.at[1 + o])
        return copies, own

    first = [stage1(o) for o in range(OPS)]

    half = rows // 2
    tau_copies = {}

    def tau_rows(index, start=0, size=rows):
        return tau.at[:, pl.ds(pl.multiple_of(index * rows + start, 16), size), :]

    def pass_on(name, src, dst, device):
        k = len(tau_copies)
        copy = remote(src, dst, tau_send.at[k], tau_recv.at[k], device)
        copy.start()
        tau_copies[name] = copy

    def pass_rows(name, index, device, start=0, size=rows):
        ref = tau_rows(index, start, size)
        pass_on(name, ref, ref, device)

    zp, zm, zf = (z + 1) % 4, (z + 3) % 4, (z + 2) % 4
    up, down, sibling = at_mode(yl, zp, core), at_mode(yl, zm, core), at_mode(yl, z, 1 - core)
    own_chunk = chunk(yl, z, core)

    for copy in first[0][0]:
        copy.start()
    first[0][1].start()
    pass_on("y", prop, tau_rows(own_chunk), at_mode(1 - yl, z, core))
    pass_on("z+", prop, tau_rows(own_chunk), up)
    pass_on("z-", prop, tau_rows(own_chunk), down)
    pass_on("c", prop, tau_rows(own_chunk), sibling)
    own_tau = pltpu.make_async_copy(prop, tau_rows(own_chunk), local.at[1 + OPS])
    own_tau.start()
    for o in range(1, OPS):
        for copy in first[o][0]:
            copy.start()
        first[o][1].start()

    plane = pl.ds(yh * XS, XS)
    across = [
        remote(gathered[o].at[plane], gathered[o].at[plane], y_send.at[o], y_recv.at[o], y_partner)
        for o in range(OPS)
    ]

    def stage2(o):
        copies, own = first[o]
        own.wait()
        for copy in copies:
            copy.wait_recv()
        across[o].start()

    second = {}

    def stage3(o):
        across[o].wait_recv()
        for k, held in ((1, w_source), (0, w_sink)):
            for s in (2, 1, 3):
                slot = want_smem[(x + s) % XS, k, 0]
                staged[o, k, s - 1] = gathered[o][slot]
                copy = remote(
                    staged.at[o, k, s - 1], held.at[o, :, :, columns(x)],
                    p2_send.at[o, k, s - 1], p2_recv.at[o, k, s - 1], at_x(s))
                copy.start()
                second[o, k, s] = copy
            held[o, :, :, columns(x)] = gathered[o][want_smem[x, k, 0]]

    def wait_stage3(o, k):
        for s in range(1, XS):
            second[o, k, s].wait_recv()

    def relay(letter, y_at):
        tau_copies[letter + "z+"].wait_recv()
        below = chunk(y_at, zm, core)
        pass_rows(letter + "h+", below, up, 0, half)
        pass_rows(letter + "cz+", below, sibling)
        tau_copies[letter + "z-"].wait_recv()
        above = chunk(y_at, zp, core)
        pass_rows(letter + "h-", above, down, half, half)
        pass_rows(letter + "cz-", above, sibling)

    def relay_far(letter, y_at):
        far = chunk(y_at, zf, core)
        tau_copies[letter + "h+"].wait_recv()
        pass_rows(letter + "ch+", far, sibling, 0, half)
        tau_copies[letter + "h-"].wait_recv()
        pass_rows(letter + "ch-", far, sibling, half, half)

    stage2(0)
    own_want.wait()
    for copy in want_copies:
        copy.wait_recv()
    to_smem = pltpu.make_async_copy(want_all, want_smem, local.at[0])
    to_smem.start()
    stage2(1)
    tau_copies["y"].wait_recv()
    other = chunk(1 - yl, z, core)
    pass_rows("Vz+", other, up)
    pass_rows("Vz-", other, down)
    pass_rows("Vc", other, sibling)
    relay("", yl)
    stage2(2)
    to_smem.wait()
    stage3(0)
    relay_far("", yl)
    stage2(3)
    relay("V", 1 - yl)
    stage3(1)
    relay_far("V", 1 - yl)
    stage3(2)
    own_tau.wait()
    for name in ("c", "Vc", "cz+", "cz-", "Vcz+", "Vcz-", "ch+", "ch-", "Vch+", "Vch-"):
        tau_copies[name].wait_recv()

    span = 4 * rows
    dims = (((1,), (1,)), ((), ()))

    def source(h):
        for j in range(2):
            o = 2 * h + j
            wait_stage3(o, 1)
            real, imag = w_source[o, 0], w_source[o, 1]
            stack[pl.ds(2 * j * rows, rows), :] = real
            stack[pl.ds((2 * j + 1) * rows, rows), :] = -imag
            stack2[pl.ds(2 * j * rows, rows), :] = imag
            stack2[pl.ds((2 * j + 1) * rows, rows), :] = real

        @pl.loop(0, order // span)
        def _(i):
            at = pl.ds(pl.multiple_of(i * span, 16), span)
            total = lax.dot_general(tau[0, at, :], stack[...], dims, preferred_element_type=F32)
            total += lax.dot_general(tau[1, at, :], stack2[...], dims, preferred_element_type=F32)
            turned[h, pl.ds(i * 4, 4)] = total.astype(BF16).reshape(4, rows, span)

        @pl.loop(1, MODES)
        def _(step):
            to = (mode + step) % MODES
            remote(turned.at[h, to], arrived.at[h, mode],
                   t_send.at[h, step], t_recv.at[h, step], (pair, to)).start()

        pltpu.make_async_copy(turned.at[h, mode], arrived.at[h, mode], local.at[2 + OPS + h]).start()

    def wait_source(h):
        pltpu.make_async_copy(turned.at[h, mode], arrived.at[h, mode], local.at[2 + OPS + h]).wait()

        @pl.loop(1, MODES)
        def _(step):
            to = (mode + step) % MODES
            remote(turned.at[h, to], arrived.at[h, mode],
                   t_send.at[h, step], t_recv.at[h, step], (pair, to)).wait()

    wide = 256

    def sink_product(h):
        for j in range(2):
            o = 2 * h + j
            wait_stage3(o, 0)
            stack[pl.ds(2 * j * rows, rows), :] = -w_sink[o, 1]
            stack[pl.ds((2 * j + 1) * rows, rows), :] = w_sink[o, 0]

        @pl.loop(0, order // wide)
        def _(i):
            at = pl.ds(pl.multiple_of(i * wide, 128), wide)
            left = w_sink[2 * h:2 * h + 2].reshape(span, order)
            total = jnp.dot(left, tau[0, :, at], preferred_element_type=F32)
            total += jnp.dot(stack[...], tau[1, :, at], preferred_element_type=F32)
            sink[2 * h:2 * h + 2, :, :, at] = total.astype(BF16).reshape(2, 2, rows, wide)

        pltpu.make_async_copy(sink.at[pl.ds(2 * h, 2)], sink_hbm.at[pl.ds(2 * h, 2)], out_sem.at[h]).start()

    tall = 16

    def contract(h):
        group = lax.broadcasted_iota(jnp.int32, (tall, span), 1) // rows
        picks = [group == b for b in range(3)]

        def body(it, sums):
            sums = list(sums)
            row = pl.ds(pl.multiple_of((it // 4) * tall, tall), tall)
            g = it % 4
            blocks = [arrived[h, 4 * g + b, row, :].astype(F32) for b in range(4)]
            source_parts = []
            for a in range(4):
                moved = [
                    blocks[b] if a == b else pltpu.roll(blocks[b], (rows * (b - a)) % span, 1)
                    for b in range(4)
                ]
                source_parts.append(jnp.where(
                    picks[0], moved[0], jnp.where(picks[1], moved[1], jnp.where(picks[2], moved[2], moved[3]))))
            at = pl.ds(pl.multiple_of(g * span, 128), span)
            for o in range(OPS):
                s_re = sink[o, 0, row, at].astype(F32)
                s_im = sink[o, 1, row, at].astype(F32)
                for j in range(2):
                    t_re, t_im = source_parts[2 * j], source_parts[2 * j + 1]
                    for part, value in enumerate((s_re * t_re + s_im * t_im, s_im * t_re - s_re * t_im)):
                        value = value[:8] + value[8:]
                        value = value[:, :128] + value[:, 128:256] + value[:, 256:]
                        sums[(o * 2 + j) * 2 + part] += value
            return tuple(sums)

        zero = jnp.zeros((8, 128), F32)
        sums = lax.fori_loop(0, (rows // tall) * 4, body, (zero,) * (OPS * 4))
        for o in range(OPS):
            for j in range(2):
                for part in range(2):
                    index = (o * OPS + 2 * h + j) * 2 + part
                    parts[mode, pl.ds(index, 1), :] = jnp.sum(
                        sums[(o * 2 + j) * 2 + part], axis=0, keepdims=True)

    source(0)
    stage3(3)
    sink_product(0)
    source(1)
    sink_product(1)
    wait_source(0)
    contract(0)
    wait_source(1)
    contract(1)

    @pl.loop(1, MODES)
    def _(step):
        remote(parts.at[mode], parts.at[mode], ps_send.at[step], ps_recv.at[step],
               (pair, (mode + step) % MODES)).start()

    @pl.loop(1, MODES)
    def _(step):
        remote(parts.at[mode], parts.at[mode], ps_send.at[step], ps_recv.at[step],
               (pair, (mode + step) % MODES)).wait()

    total = parts[0]
    for n in range(1, MODES):
        total = total + parts[n]
    total = jnp.sum(total, axis=1, keepdims=True) * (1.0 / order)
    corr_ref[...] = jnp.broadcast_to(total, corr_ref.shape)

    for copy in want_copies:
        copy.wait_send()
    for copies, _ in first:
        for copy in copies:
            copy.wait_send()
    for copy in across:
        copy.wait_send()
    for copy in second.values():
        copy.wait_send()
    for copy in tau_copies.values():
        copy.wait_send()
    for h in range(2):
        pltpu.make_async_copy(sink.at[pl.ds(2 * h, 2)], sink_hbm.at[pl.ds(2 * h, 2)], out_sem.at[h]).wait()


def body(time_pairs, slot_of, elementals, propagators):
    _, ops, parts, rows, order = elementals.shape
    slots = slot_of.shape[0]
    positions = jnp.arange(slots, dtype=jnp.int32)
    wanted = jnp.sum(
        jnp.where(time_pairs.reshape(-1)[:, None] == positions[None, :], slot_of[None, :], 0), axis=1
    )
    line = lax.broadcasted_iota(jnp.int32, (8, 128), 0)
    want = jnp.where(line == 0, wanted[0], wanted[1]).astype(jnp.int32)
    quarter = order // XS
    dma = pltpu.SemaphoreType.DMA
    sink, corr = pl.pallas_call(
        kernel,
        out_shape=(
            jax.ShapeDtypeStruct((ops, 2, rows, order), BF16),
            jax.ShapeDtypeStruct((ops * ops * 2, 128), F32),
        ),
        in_specs=[
            pl.BlockSpec(memory_space=pltpu.VMEM),
            pl.BlockSpec(memory_space=pl.ANY),
            pl.BlockSpec(memory_space=pl.ANY),
        ],
        out_specs=(pl.BlockSpec(memory_space=pl.ANY), pl.BlockSpec(memory_space=pltpu.VMEM)),
        scratch_shapes=[
            *[pltpu.VMEM((slots, 2, rows, quarter), BF16)] * OPS,
            pltpu.VMEM((ops, 2, XS - 1, 2, rows, quarter), BF16),
            pltpu.VMEM((ops, 2, rows, order), BF16),
            pltpu.VMEM((ops, 2, rows, order), BF16),
            pltpu.VMEM((2, order, order), BF16),
            pltpu.VMEM((4 * rows, order), BF16),
            pltpu.VMEM((4 * rows, order), BF16),
            pltpu.VMEM((2, MODES, rows, 4 * rows), BF16),
            pltpu.VMEM((2, MODES, rows, 4 * rows), BF16),
            pltpu.VMEM((ops, 2, rows, order), BF16),
            pltpu.VMEM((XS, 8, 128), jnp.int32),
            pltpu.SMEM((XS, 8, 128), jnp.int32),
            pltpu.VMEM((MODES, ops * ops * 2, 128), F32),
            dma((XS - 1,)), dma((XS - 1,)),
            dma((OPS, XS - 1)), dma((OPS, XS - 1)),
            dma((OPS,)), dma((OPS,)),
            dma((OPS, 2, XS - 1)), dma((OPS, 2, XS - 1)),
            dma((24,)), dma((24,)),
            dma((2, MODES)), dma((2, MODES)),
            dma((MODES,)), dma((MODES,)),
            dma((2 + OPS + 2,)), dma((2,)),
        ],
        compiler_params=pltpu.CompilerParams(
            collective_id=0, has_side_effects=True, vmem_limit_bytes=56 << 20
        ),
        name="meson",
    )(want, elementals[0], propagators[0])
    return corr[:, 0].reshape(1, ops, ops, 2), sink[None]


def solution(mesh):
    in_specs = (
        P("pair", None),
        P(),
        P("pair", None, None, "mode", None),
        P("pair", None, "mode", None),
    )
    out_specs = (P("pair", None, None, None), P("pair", None, None, "mode", None))
    return jax.shard_map(body, mesh=mesh, in_specs=in_specs, out_specs=out_specs, check_vma=False)
```

time: 398 us -> 126 us (0.32)
  waiting for transfers between devices: 259 us -> 0 us
  Pallas kernels: 0 us -> 117 us
  matrix products: 41.1 us -> 0 us
  local copies, waits for them, and re-layouts: 42.7 us -> 6.1 us
  blocking collectives: 31.6 us -> 0 us
  between operations: 14.3 us -> 0.65 us
  starting transfers between devices: 5.32 us -> 0 us
    all_gather x2 -> x0, waiting for transfers between devices: 233 us -> none  [the longest x1 209 us: body(): segment = lax.all_gather(elementals, 'pair', axis=0, tiled=True)]
    pallas_call x0 -> x1, Pallas kernels: none -> 117 us  [body(): pl.pallas_call(kernel, out_shape=(jax.ShapeDtypeStruct((ops, 2, rows, ord...]
    dot_general x13 -> x0, matrix products: 41.1 us -> none  [the longest x1 9.68 us: body(): jnp.dot(match.astype(jnp.bfloat16), segment.reshape(count, slab_size), pr...]
    psum x1 -> x0, blocking collectives: 31.6 us -> none  [body(): totals = lax.psum(partials, 'mode')]
    all_to_all x1 -> x0, waiting for transfers between devices: 24.4 us -> none  [body(): lax.all_to_all(turned, 'mode', split_axis=3, concat_axis=2, tiled=True)]
    unnamed x28 -> x2, local copies, waits for them, and re-layouts: 27 us -> 3.93 us
    all_to_all x2 -> x0, local copies, waits for them, and re-layouts: 11.7 us -> none  [body(): lax.all_to_all(turned, 'mode', split_axis=3, concat_axis=2, tiled=True)]
    all_to_all x1 -> x0, starting transfers between devices: 5.25 us -> none  [body(): lax.all_to_all(turned, 'mode', split_axis=3, concat_axis=2, tiled=True)]
  transfers between devices with their start and end apart: 3 -> 0, of which waited for: 3 -> 0; matrix products, arithmetic and copies ran while one was open for 12% -> 0% of each run, Pallas kernels for 0% -> 0%
where the time goes in v1:
time: 126 us
  Pallas kernels  117 us (93%)
  local copies, waits for them, and re-layouts  6.1 us (5%)
  other arithmetic  2.15 us (2%)
    pallas_call x1, Pallas kernels, body(): pl.pallas_call(kernel, out_shape=(jax.ShapeDtypeStruct((ops, 2, rows, ord...  117 us
    unnamed x2, local copies, waits for them, and re-layouts  3.93 us

profile of v1, /device:TPU:1, one launch (start us, length us, event | category | flops | bytes accessed | tf_op | source)
XLA Modules:
  0.0 126.2 jit_solution(17744133031440733017)
XLA Ops:
  0.6 0.9 fusion
  1.5 0.6 fusion.1
  2.1 1.3 %compare_select_fusion.1 = s32[8]{0:T(128)S(1)} fusion(s32[]{:T(128)} %bitcast.2, s32[]{:T(128)} %bitcast.1), kind=kLoop, calls=%fused_computation.2 | loop fusion | flops 16 | bytes 40 | tf_op jit(solution)/shard_map/jit(_where)/select_n | solution.py:336
  3.4 0.7 iota.11.want_ref
  4.0 117.3 %meson.1 = (bf16[4,2,96,1536]{3,2,1,0:T(8,128)(2,1)}, f32[32,128]{1,0:T(8,128)}) custom-call(s32[8,128]{1,0:T(8,128)} %iota.11.want_ref, bf16[4,2,96,1536]{3,2,1,0:T(8,128)(2,1)} %bitcast.6, bf16[2,96,1536]{2,1,0:T(8,128)(2,1)} %bitcast.8), custom_call_target="tpu_custom_call" | custom-call | tf_op jit(solution)/shard_map/meson/pallas_call | solution.py:339
  121.4 0.8 slice_reduce_fusion
  122.2 0.1 reshape_squeeze.3
  122.3 0.7 copy.8
  123.0 3.2 %copy.10 = bf16[1,4,2,96,1536]{4,3,2,1,0:T(8,128)(2,1)} copy(bf16[1,4,2,96,1536]{4,3,2,1,0:T(8,128)(2,1)} %bitcast.7) | data formatting | bytes 4718592

commit v2 on v1

--- a/solution.py
+++ b/solution.py
@@ -14,11 +14,12 @@
 SLOTS = 8
 
 
-def kernel(want_ref, elem, prop, sink_hbm, corr_ref,
+def kernel(times, slots, elem_ref, prop_ref, sink_ref, corr_ref,
            r0, r1, r2, r3, staged, w_sink, w_source, tau, stack, stack2, turned, arrived, sink,
            want_all, want_smem, parts,
            want_send, want_recv, p1_send, p1_recv, y_send, y_recv, p2_send, p2_recv,
            tau_send, tau_recv, t_send, t_recv, ps_send, ps_recv, local, out_sem):
+    elem, prop, sink_hbm = elem_ref.at[0], prop_ref.at[0], sink_ref.at[0]
     rows = elem.shape[2]
     order = elem.shape[3]
     quarter = order // XS
@@ -45,6 +46,9 @@
             src_ref=src, dst_ref=dst, send_sem=send, recv_sem=recv,
             device_id=device, device_id_type=MESH)
 
+    line = lax.broadcasted_iota(jnp.int32, (8, 128), 0)
+    want_all[x] = jnp.where(line == 0, slots[times[0, 0]], slots[times[0, 1]])
+
     barrier = pltpu.get_barrier_semaphore()
     for step in range(1, XS):
         pl.semaphore_signal(barrier, inc=1, device_id=at_x(step), device_id_type=MESH)
@@ -57,13 +61,11 @@
     pl.semaphore_wait(barrier, XS - 1 + 1 + MODES - 1)
 
     want_copies = [
-        remote(want_ref, want_all.at[x], want_send.at[s - 1], want_recv.at[s - 1], at_x(s))
+        remote(want_all.at[x], want_all.at[x], want_send.at[s - 1], want_recv.at[s - 1], at_x(s))
         for s in range(1, XS)
     ]
     for copy in want_copies:
         copy.start()
-    own_want = pltpu.make_async_copy(want_ref, want_all.at[x], local.at[0])
-    own_want.start()
 
     def columns(at):
         return pl.ds(pl.multiple_of(at * quarter, 128), quarter)
@@ -163,7 +165,6 @@
         pass_rows(letter + "ch-", far, sibling, half, half)
 
     stage2(0)
-    own_want.wait()
     for copy in want_copies:
         copy.wait_recv()
     to_smem = pltpu.make_async_copy(want_all, want_smem, local.at[0])
@@ -280,7 +281,7 @@
         for o in range(OPS):
             for j in range(2):
                 for part in range(2):
-                    index = (o * OPS + 2 * h + j) * 2 + part
+                    index = (o * 2 + part) * OPS + 2 * h + j
                     parts[mode, pl.ds(index, 1), :] = jnp.sum(
                         sums[(o * 2 + j) * 2 + part], axis=0, keepdims=True)
 
@@ -308,7 +309,11 @@
     for n in range(1, MODES):
         total = total + parts[n]
     total = jnp.sum(total, axis=1, keepdims=True) * (1.0 / order)
-    corr_ref[...] = jnp.broadcast_to(total, corr_ref.shape)
+    total = jnp.broadcast_to(total, parts.shape[1:])
+    lane = lax.broadcasted_iota(jnp.int32, (OPS, 2), 1)
+    for o in range(OPS):
+        at = 2 * OPS * o
+        corr_ref[0, o] = jnp.where(lane == 0, total[at:at + OPS, :2], total[at + OPS:at + 2 * OPS, :2])
 
     for copy in want_copies:
         copy.wait_send()
@@ -328,22 +333,17 @@
 def body(time_pairs, slot_of, elementals, propagators):
     _, ops, parts, rows, order = elementals.shape
     slots = slot_of.shape[0]
-    positions = jnp.arange(slots, dtype=jnp.int32)
-    wanted = jnp.sum(
-        jnp.where(time_pairs.reshape(-1)[:, None] == positions[None, :], slot_of[None, :], 0), axis=1
-    )
-    line = lax.broadcasted_iota(jnp.int32, (8, 128), 0)
-    want = jnp.where(line == 0, wanted[0], wanted[1]).astype(jnp.int32)
     quarter = order // XS
     dma = pltpu.SemaphoreType.DMA
     sink, corr = pl.pallas_call(
         kernel,
         out_shape=(
-            jax.ShapeDtypeStruct((ops, 2, rows, order), BF16),
-            jax.ShapeDtypeStruct((ops * ops * 2, 128), F32),
+            jax.ShapeDtypeStruct(elementals.shape, BF16),
+            jax.ShapeDtypeStruct((1, ops, ops, 2), F32),
         ),
         in_specs=[
-            pl.BlockSpec(memory_space=pltpu.VMEM),
+            pl.BlockSpec(memory_space=pltpu.SMEM),
+            pl.BlockSpec(memory_space=pltpu.SMEM),
             pl.BlockSpec(memory_space=pl.ANY),
             pl.BlockSpec(memory_space=pl.ANY),
         ],
@@ -375,8 +375,8 @@
             collective_id=0, has_side_effects=True, vmem_limit_bytes=56 << 20
         ),
         name="meson",
-    )(want, elementals[0], propagators[0])
-    return corr[:, 0].reshape(1, ops, ops, 2), sink[None]
+    )(time_pairs, slot_of, elementals, propagators)
+    return corr, sink
 
 
 def solution(mesh):

time: 126 us -> 123 us (0.976)
  other arithmetic: 2.15 us -> 0 us
  local copies, waits for them, and re-layouts: 6.1 us -> 4.61 us
    slice x2 -> x0, local copies, waits for them, and re-layouts: 1.41 us -> none  [the longest x1 0.83 us: body(): return (corr[:, 0].reshape(1, ops, ops, 2), sink[None])]
    select_n x1 -> x0, other arithmetic: 1.29 us -> none  [body(): want = jnp.where(line == 0, wanted[0], wanted[1]).astype(jnp.int32)]
where the time goes in v2:
time: 123 us
  Pallas kernels  117 us (95%)
  local copies, waits for them, and re-layouts  4.61 us (4%)
    pallas_call x1, Pallas kernels, body(): pl.pallas_call(kernel, out_shape=(jax.ShapeDtypeStruct(elementals.shape,...  117 us
    unnamed x2, local copies, waits for them, and re-layouts  4.61 us

profile of v2, /device:TPU:1, one launch (start us, length us, event | category | flops | bytes accessed | tf_op | source)
XLA Modules:
  0.0 122.7 jit_solution(2681200792477415958)
XLA Ops:
  0.6 117.5 %meson.1 = (bf16[1,4,2,96,1536]{4,3,2,1,0:T(8,128)(2,1)}, f32[1,4,4,2]{3,2,1,0:T(4,128)}) custom-call(s32[1,2]{1,0:T(1,128)} %times.1, s32[8]{0:T(128)} %slots.1, bf16[1,4,2,96,1536]{4,3,2,1,0:T(8,128)(2,1)} %elem_ref.1, bf16[1,2,96,1536]{3,2,1,0:T(8,128)(2,1)} %prop_ref.1), custom_call_target="tpu_custom_call" | custom-call | tf_op jit(solution)/shard_map/meson/pallas_call | solution.py:338
  118.1 1.4 %copy.6 = f32[1,4,4,2]{2,3,1,0:T(2,128)} copy(f32[1,4,4,2]{3,2,1,0:T(4,128)} %get-tuple-element.6) | data formatting | bytes 256
  119.5 3.2 %copy.8 = bf16[1,4,2,96,1536]{4,3,2,1,0:T(8,128)(2,1)} copy(bf16[1,4,2,96,1536]{4,3,2,1,0:T(8,128)(2,1)} %get-tuple-element.11) | data formatting | bytes 4718592

commit v3 on v2

--- a/solution.py
+++ b/solution.py
@@ -1,3 +1,5 @@
+import functools
+
 import jax
 import jax.numpy as jnp
 from jax import lax
@@ -16,7 +18,7 @@
 
 def kernel(times, slots, elem_ref, prop_ref, sink_ref, corr_ref,
            r0, r1, r2, r3, staged, w_sink, w_source, tau, stack, stack2, turned, arrived, sink,
-           want_all, want_smem, parts,
+           want_all, want_smem, lines, parts,
            want_send, want_recv, p1_send, p1_recv, y_send, y_recv, p2_send, p2_recv,
            tau_send, tau_recv, t_send, t_recv, ps_send, ps_recv, local, out_sem):
     elem, prop, sink_hbm = elem_ref.at[0], prop_ref.at[0], sink_ref.at[0]
@@ -203,28 +205,26 @@
             stack2[pl.ds((2 * j + 1) * rows, rows), :] = real
 
         @pl.loop(0, order // span)
-        def _(i):
+        def _(step):
+            i = (step + mode // 4 + 1) % 4
             at = pl.ds(pl.multiple_of(i * span, 16), span)
             total = lax.dot_general(tau[0, at, :], stack[...], dims, preferred_element_type=F32)
             total += lax.dot_general(tau[1, at, :], stack2[...], dims, preferred_element_type=F32)
             turned[h, pl.ds(i * 4, 4)] = total.astype(BF16).reshape(4, rows, span)
 
-        @pl.loop(1, MODES)
-        def _(step):
-            to = (mode + step) % MODES
-            remote(turned.at[h, to], arrived.at[h, mode],
-                   t_send.at[h, step], t_recv.at[h, step], (pair, to)).start()
-
-        pltpu.make_async_copy(turned.at[h, mode], arrived.at[h, mode], local.at[2 + OPS + h]).start()
-
-    def wait_source(h):
-        pltpu.make_async_copy(turned.at[h, mode], arrived.at[h, mode], local.at[2 + OPS + h]).wait()
-
-        @pl.loop(1, MODES)
-        def _(step):
-            to = (mode + step) % MODES
-            remote(turned.at[h, to], arrived.at[h, mode],
-                   t_send.at[h, step], t_recv.at[h, step], (pair, to)).wait()
+            @pl.loop(i * 4, i * 4 + 4)
+            def _(to):
+                @pl.when(to != mode)
+                def _():
+                    slab(h, to, mode).start()
+
+        own_slab(h).start()
+
+    def slab(h, to, sender):
+        return remote(turned.at[h, to], arrived.at[h, sender], t_send.at[h, to], t_recv.at[h, sender], (pair, to))
+
+    def own_slab(h):
+        return pltpu.make_async_copy(turned.at[h, mode], arrived.at[h, mode], local.at[2 + OPS + h])
 
     wide = 256
 
@@ -251,10 +251,9 @@
         group = lax.broadcasted_iota(jnp.int32, (tall, span), 1) // rows
         picks = [group == b for b in range(3)]
 
-        def body(it, sums):
+        def body(g, it, sums):
             sums = list(sums)
-            row = pl.ds(pl.multiple_of((it // 4) * tall, tall), tall)
-            g = it % 4
+            row = pl.ds(pl.multiple_of(it * tall, tall), tall)
             blocks = [arrived[h, 4 * g + b, row, :].astype(F32) for b in range(4)]
             source_parts = []
             for a in range(4):
@@ -276,13 +275,25 @@
                         sums[(o * 2 + j) * 2 + part] += value
             return tuple(sums)
 
+        def from_group(step, sums):
+            g = (mode // 4 + step) % 4
+
+            @pl.loop(4 * g, 4 * g + 4)
+            def _(sender):
+                @pl.when(sender != mode)
+                def _():
+                    slab(h, sender, sender).wait_recv()
+
+            return lax.fori_loop(0, rows // tall, functools.partial(body, g), sums)
+
+        own_slab(h).wait()
         zero = jnp.zeros((8, 128), F32)
-        sums = lax.fori_loop(0, (rows // tall) * 4, body, (zero,) * (OPS * 4))
+        sums = lax.fori_loop(0, MODES // 4, from_group, (zero,) * (OPS * 4))
         for o in range(OPS):
             for j in range(2):
                 for part in range(2):
-                    index = (o * 2 + part) * OPS + 2 * h + j
-                    parts[mode, pl.ds(index, 1), :] = jnp.sum(
+                    index = (2 * h + j) * 2 * OPS + 2 * o + part
+                    lines[index:index + 1, :] = jnp.sum(
                         sums[(o * 2 + j) * 2 + part], axis=0, keepdims=True)
 
     source(0)
@@ -290,10 +301,15 @@
     sink_product(0)
     source(1)
     sink_product(1)
-    wait_source(0)
     contract(0)
-    wait_source(1)
     contract(1)
+
+    column = jnp.sum(lines[...], axis=1, keepdims=True)
+    lane = lax.broadcasted_iota(jnp.int32, (2 * OPS, 128), 1)
+    tile = jnp.zeros((2 * OPS, 128), F32)
+    for q in range(OPS):
+        tile = jnp.where(lane == q, column[2 * OPS * q:2 * OPS * (q + 1)], tile)
+    parts[mode] = tile
 
     @pl.loop(1, MODES)
     def _(step):
@@ -308,12 +324,9 @@
     total = parts[0]
     for n in range(1, MODES):
         total = total + parts[n]
-    total = jnp.sum(total, axis=1, keepdims=True) * (1.0 / order)
-    total = jnp.broadcast_to(total, parts.shape[1:])
-    lane = lax.broadcasted_iota(jnp.int32, (OPS, 2), 1)
+    total = total * (1.0 / order)
     for o in range(OPS):
-        at = 2 * OPS * o
-        corr_ref[0, o] = jnp.where(lane == 0, total[at:at + OPS, :2], total[at + OPS:at + 2 * OPS, :2])
+        corr_ref[0, o] = total[2 * o:2 * o + 2, :OPS]
 
     for copy in want_copies:
         copy.wait_send()
@@ -327,6 +340,13 @@
     for copy in tau_copies.values():
         copy.wait_send()
     for h in range(2):
+        @pl.loop(0, MODES)
+        def _(to):
+            @pl.when(to != mode)
+            def _():
+                slab(h, to, mode).wait_send()
+
+    for h in range(2):
         pltpu.make_async_copy(sink.at[pl.ds(2 * h, 2)], sink_hbm.at[pl.ds(2 * h, 2)], out_sem.at[h]).wait()
 
 
@@ -339,7 +359,7 @@
         kernel,
         out_shape=(
             jax.ShapeDtypeStruct(elementals.shape, BF16),
-            jax.ShapeDtypeStruct((1, ops, ops, 2), F32),
+            jax.ShapeDtypeStruct((1, ops, 2, ops), F32),
         ),
         in_specs=[
             pl.BlockSpec(memory_space=pltpu.SMEM),
@@ -361,7 +381,8 @@
             pltpu.VMEM((ops, 2, rows, order), BF16),
             pltpu.VMEM((XS, 8, 128), jnp.int32),
             pltpu.SMEM((XS, 8, 128), jnp.int32),
-            pltpu.VMEM((MODES, ops * ops * 2, 128), F32),
+            pltpu.VMEM((ops * ops * 2, 128), F32),
+            pltpu.VMEM((MODES, 2 * ops, 128), F32),
             dma((XS - 1,)), dma((XS - 1,)),
             dma((OPS, XS - 1)), dma((OPS, XS - 1)),
             dma((OPS,)), dma((OPS,)),
@@ -376,7 +397,7 @@
         ),
         name="meson",
     )(time_pairs, slot_of, elementals, propagators)
-    return corr, sink
+    return jnp.swapaxes(corr, 2, 3), sink
 
 
 def solution(mesh):

time: 123 us -> 119 us (0.967)
  Pallas kernels: 117 us -> 113 us
    pallas_call x1, Pallas kernels: 117 us -> 113 us  [body(): pl.pallas_call(kernel, out_shape=(jax.ShapeDtypeStruct(elementals.shape,...]
where the time goes in v3:
time: 119 us; the launch traced here: 118 us
  Pallas kernels  113 us (95%)
  local copies, waits for them, and re-layouts  4.49 us (4%)
    pallas_call x1, Pallas kernels, body(): pl.pallas_call(kernel, out_shape=(jax.ShapeDtypeStruct(elementals.shape,...  113 us
    unnamed x2, local copies, waits for them, and re-layouts  4.49 us

profile of v3, /device:TPU:1, one launch (start us, length us, event | category | flops | bytes accessed | tf_op | source)
XLA Modules:
  0.0 118.3 jit_solution(2383055935641656549)
XLA Ops:
  0.6 113.2 %meson.1 = (bf16[1,4,2,96,1536]{4,3,2,1,0:T(8,128)(2,1)}, f32[1,4,2,4]{3,2,1,0:T(2,128)}) custom-call(s32[1,2]{1,0:T(1,128)} %times.1, s32[8]{0:T(128)} %slots.1, bf16[1,4,2,96,1536]{4,3,2,1,0:T(8,128)(2,1)} %elem_ref.1, bf16[1,2,96,1536]{3,2,1,0:T(8,128)(2,1)} %prop_ref.1), custom_call_target="tpu_custom_call" | custom-call | tf_op jit(solution)/shard_map/meson/pallas_call | solution.py:358
  113.8 1.3 %copy.8 = f32[1,4,4,2]{2,3,1,0:T(2,128)} copy(f32[1,4,4,2]{2,3,1,0:T(2,128)} %bitcast.1) | data formatting | bytes 256
  115.1 3.2 %copy.9 = bf16[1,4,2,96,1536]{4,3,2,1,0:T(8,128)(2,1)} copy(bf16[1,4,2,96,1536]{4,3,2,1,0:T(8,128)(2,1)} %get-tuple-element.9) | data formatting | bytes 4718592

commit v4 on v3

--- a/solution.py
+++ b/solution.py
@@ -1,5 +1,3 @@
-import functools
-
 import jax
 import jax.numpy as jnp
 from jax import lax
@@ -17,11 +15,11 @@
 
 
 def kernel(times, slots, elem_ref, prop_ref, sink_ref, corr_ref,
-           r0, r1, r2, r3, staged, w_sink, w_source, tau, stack, stack2, turned, arrived, sink,
+           r0, r1, r2, r3, staged, w_sink, w_source, tau, stack, stack2, left, turned, arrived, aligned,
            want_all, want_smem, lines, parts,
            want_send, want_recv, p1_send, p1_recv, y_send, y_recv, p2_send, p2_recv,
-           tau_send, tau_recv, t_send, t_recv, ps_send, ps_recv, local, out_sem):
-    elem, prop, sink_hbm = elem_ref.at[0], prop_ref.at[0], sink_ref.at[0]
+           tau_send, tau_recv, t_send, t_recv, ps_send, ps_recv, local):
+    elem, prop, sink = elem_ref.at[0], prop_ref.at[0], sink_ref.at[0]
     rows = elem.shape[2]
     order = elem.shape[3]
     quarter = order // XS
@@ -193,116 +191,141 @@
 
     span = 4 * rows
     dims = (((1,), (1,)), ((), ()))
-
-    def source(h):
-        for j in range(2):
-            o = 2 * h + j
-            wait_stage3(o, 1)
-            real, imag = w_source[o, 0], w_source[o, 1]
-            stack[pl.ds(2 * j * rows, rows), :] = real
-            stack[pl.ds((2 * j + 1) * rows, rows), :] = -imag
-            stack2[pl.ds(2 * j * rows, rows), :] = imag
-            stack2[pl.ds((2 * j + 1) * rows, rows), :] = real
-
-        @pl.loop(0, order // span)
-        def _(step):
-            i = (step + mode // 4 + 1) % 4
-            at = pl.ds(pl.multiple_of(i * span, 16), span)
+    pad = stack.shape[0] - 2 * rows
+    stack[pl.ds(2 * rows, pad), :] = jnp.zeros((pad, order), BF16)
+    stack2[pl.ds(2 * rows, pad), :] = jnp.zeros((pad, order), BF16)
+
+    def slab(o, to, sender):
+        return remote(turned.at[o, to], arrived.at[o, sender], t_send.at[o, to], t_recv.at[o, sender], (pair, to))
+
+    def own_slab(o):
+        return pltpu.make_async_copy(turned.at[o, mode], arrived.at[o, mode], local.at[2 + OPS + o])
+
+    def source(o):
+        wait_stage3(o, 1)
+        real, imag = w_source[o, 0], w_source[o, 1]
+        stack[pl.ds(0, rows), :] = real
+        stack[pl.ds(rows, rows), :] = -imag
+        stack2[pl.ds(0, rows), :] = imag
+        stack2[pl.ds(rows, rows), :] = real
+
+        blocks = 2 if o == OPS - 1 else 1
+        many = order // blocks
+        owners = MODES // blocks
+
+        @pl.loop(0, blocks)
+        def _(i):
+            at = pl.ds(pl.multiple_of(i * many, 16), many)
             total = lax.dot_general(tau[0, at, :], stack[...], dims, preferred_element_type=F32)
             total += lax.dot_general(tau[1, at, :], stack2[...], dims, preferred_element_type=F32)
-            turned[h, pl.ds(i * 4, 4)] = total.astype(BF16).reshape(4, rows, span)
-
-            @pl.loop(i * 4, i * 4 + 4)
-            def _(to):
+            total = total.reshape(owners, 2, half, 2 * rows + pad)
+            blank = jnp.zeros((owners * half, span - 2 * rows - pad), F32)
+            upper = jnp.concatenate([total[:, 0].reshape(owners * half, 2 * rows + pad), blank], axis=1)
+            lower = jnp.concatenate([blank, total[:, 1].reshape(owners * half, 2 * rows + pad)], axis=1)
+            packed = upper + pltpu.roll(lower, pad, 1)
+            turned[o, pl.ds(i * owners, owners)] = packed.astype(BF16).reshape(owners, half, span)
+
+            @pl.loop(0, owners)
+            def _(step):
+                to = i * owners + (mode + step) % owners
+
                 @pl.when(to != mode)
                 def _():
-                    slab(h, to, mode).start()
-
-        own_slab(h).start()
-
-    def slab(h, to, sender):
-        return remote(turned.at[h, to], arrived.at[h, sender], t_send.at[h, to], t_recv.at[h, sender], (pair, to))
-
-    def own_slab(h):
-        return pltpu.make_async_copy(turned.at[h, mode], arrived.at[h, mode], local.at[2 + OPS + h])
-
-    wide = 256
-
-    def sink_product(h):
-        for j in range(2):
-            o = 2 * h + j
-            wait_stage3(o, 0)
-            stack[pl.ds(2 * j * rows, rows), :] = -w_sink[o, 1]
-            stack[pl.ds((2 * j + 1) * rows, rows), :] = w_sink[o, 0]
+                    slab(o, to, mode).start()
+
+        own_slab(o).start()
+
+    wide = 768
+
+    def sink_product(o):
+        wait_stage3(o, 0)
+        left[pl.ds(0, rows), pl.ds(0, order)] = w_sink[o, 0]
+        left[pl.ds(0, rows), pl.ds(order, order)] = -w_sink[o, 1]
+        left[pl.ds(rows, rows), pl.ds(0, order)] = w_sink[o, 1]
+        left[pl.ds(rows, rows), pl.ds(order, order)] = w_sink[o, 0]
 
         @pl.loop(0, order // wide)
         def _(i):
             at = pl.ds(pl.multiple_of(i * wide, 128), wide)
-            left = w_sink[2 * h:2 * h + 2].reshape(span, order)
-            total = jnp.dot(left, tau[0, :, at], preferred_element_type=F32)
-            total += jnp.dot(stack[...], tau[1, :, at], preferred_element_type=F32)
-            sink[2 * h:2 * h + 2, :, :, at] = total.astype(BF16).reshape(2, 2, rows, wide)
-
-        pltpu.make_async_copy(sink.at[pl.ds(2 * h, 2)], sink_hbm.at[pl.ds(2 * h, 2)], out_sem.at[h]).start()
+            total = jnp.dot(left[...], tau[:, :, at].reshape(2 * order, wide), preferred_element_type=F32)
+            sink[o, :, :, at] = total.astype(BF16).reshape(2, rows, wide)
 
     tall = 16
 
-    def contract(h):
+    def align(o):
         group = lax.broadcasted_iota(jnp.int32, (tall, span), 1) // rows
         picks = [group == b for b in range(3)]
-
-        def body(g, it, sums):
-            sums = list(sums)
-            row = pl.ds(pl.multiple_of(it * tall, tall), tall)
-            blocks = [arrived[h, 4 * g + b, row, :].astype(F32) for b in range(4)]
-            source_parts = []
-            for a in range(4):
-                moved = [
-                    blocks[b] if a == b else pltpu.roll(blocks[b], (rows * (b - a)) % span, 1)
-                    for b in range(4)
-                ]
-                source_parts.append(jnp.where(
-                    picks[0], moved[0], jnp.where(picks[1], moved[1], jnp.where(picks[2], moved[2], moved[3]))))
-            at = pl.ds(pl.multiple_of(g * span, 128), span)
-            for o in range(OPS):
-                s_re = sink[o, 0, row, at].astype(F32)
-                s_im = sink[o, 1, row, at].astype(F32)
-                for j in range(2):
-                    t_re, t_im = source_parts[2 * j], source_parts[2 * j + 1]
-                    for part, value in enumerate((s_re * t_re + s_im * t_im, s_im * t_re - s_re * t_im)):
-                        value = value[:8] + value[8:]
-                        value = value[:, :128] + value[:, 128:256] + value[:, 256:]
-                        sums[(o * 2 + j) * 2 + part] += value
-            return tuple(sums)
-
-        def from_group(step, sums):
+        own_slab(o).wait()
+
+        @pl.loop(0, MODES // 4)
+        def _(step):
             g = (mode // 4 + step) % 4
 
             @pl.loop(4 * g, 4 * g + 4)
             def _(sender):
                 @pl.when(sender != mode)
                 def _():
-                    slab(h, sender, sender).wait_recv()
-
-            return lax.fori_loop(0, rows // tall, functools.partial(body, g), sums)
-
-        own_slab(h).wait()
+                    slab(o, sender, sender).wait_recv()
+
+            @pl.loop(0, half // tall)
+            def _(it):
+                row = pl.ds(pl.multiple_of(it * tall, tall), tall)
+                blocks = [arrived[o, 4 * g + b, row, :].astype(F32) for b in range(4)]
+                for a in range(4):
+                    moved = [
+                        blocks[b] if a == b else pltpu.roll(blocks[b], (rows * (b - a)) % span, 1)
+                        for b in range(4)
+                    ]
+                    part = jnp.where(
+                        picks[0], moved[0], jnp.where(picks[1], moved[1], jnp.where(picks[2], moved[2], moved[3])))
+                    down_to = pl.ds(pl.multiple_of((a // 2) * half + it * tall, tall), tall)
+                    aligned[o, a % 2, down_to, pl.ds(pl.multiple_of(g * span, 128), span)] = part.astype(BF16)
+
+    part_wide = 256
+
+    def contract(os, qs):
+        def body(it, sums):
+            sums = list(sums)
+            row = pl.ds(pl.multiple_of((it // 6) * tall, tall), tall)
+            at = pl.ds(pl.multiple_of((it % 6) * part_wide, 128), part_wide)
+            right = [(aligned[q, 0, row, at].astype(F32), aligned[q, 1, row, at].astype(F32)) for q in qs]
+            k = 0
+            for o in os:
+                s_re, s_im = sink[o, 0, row, at].astype(F32), sink[o, 1, row, at].astype(F32)
+                for t_re, t_im in right:
+                    for value in (s_re * t_re + s_im * t_im, s_im * t_re - s_re * t_im):
+                        value = value[:8] + value[8:]
+                        sums[k] += value[:, :128] + value[:, 128:]
+                        k += 1
+            return tuple(sums)
+
         zero = jnp.zeros((8, 128), F32)
-        sums = lax.fori_loop(0, MODES // 4, from_group, (zero,) * (OPS * 4))
-        for o in range(OPS):
-            for j in range(2):
+        sums = lax.fori_loop(0, (rows // tall) * (order // part_wide), body, (zero,) * (2 * len(os) * len(qs)))
+        k = 0
+        for o in os:
+            for q in qs:
                 for part in range(2):
-                    index = (2 * h + j) * 2 * OPS + 2 * o + part
-                    lines[index:index + 1, :] = jnp.sum(
-                        sums[(o * 2 + j) * 2 + part], axis=0, keepdims=True)
+                    index = q * 2 * OPS + 2 * o + part
+                    lines[index:index + 1, :] = jnp.sum(sums[k], axis=0, keepdims=True)
+                    k += 1
 
     source(0)
-    stage3(3)
     sink_product(0)
     source(1)
+    stage3(3)
     sink_product(1)
-    contract(0)
-    contract(1)
+    align(0)
+    source(2)
+    sink_product(2)
+    source(3)
+    align(1)
+    contract((0, 1, 2), (0, 1))
+    sink_product(3)
+    align(2)
+    contract((3,), (0, 1))
+    contract((0, 1, 2, 3), (2,))
+    align(3)
+    contract((0, 1, 2, 3), (3,))
 
     column = jnp.sum(lines[...], axis=1, keepdims=True)
     lane = lax.broadcasted_iota(jnp.int32, (2 * OPS, 128), 1)
@@ -339,15 +362,12 @@
         copy.wait_send()
     for copy in tau_copies.values():
         copy.wait_send()
-    for h in range(2):
+    for o in range(OPS):
         @pl.loop(0, MODES)
         def _(to):
             @pl.when(to != mode)
             def _():
-                slab(h, to, mode).wait_send()
-
-    for h in range(2):
-        pltpu.make_async_copy(sink.at[pl.ds(2 * h, 2)], sink_hbm.at[pl.ds(2 * h, 2)], out_sem.at[h]).wait()
+                slab(o, to, mode).wait_send()
 
 
 def body(time_pairs, slot_of, elementals, propagators):
@@ -358,8 +378,8 @@
     sink, corr = pl.pallas_call(
         kernel,
         out_shape=(
-            jax.ShapeDtypeStruct(elementals.shape, BF16),
-            jax.ShapeDtypeStruct((1, ops, 2, ops), F32),
+            pltpu.VMEM(elementals.shape, BF16),
+            pltpu.VMEM((1, ops, 2, ops), F32),
         ),
         in_specs=[
             pl.BlockSpec(memory_space=pltpu.SMEM),
@@ -367,17 +387,18 @@
             pl.BlockSpec(memory_space=pl.ANY),
             pl.BlockSpec(memory_space=pl.ANY),
         ],
-        out_specs=(pl.BlockSpec(memory_space=pl.ANY), pl.BlockSpec(memory_space=pltpu.VMEM)),
+        out_specs=(pl.BlockSpec(memory_space=pltpu.VMEM), pl.BlockSpec(memory_space=pltpu.VMEM)),
         scratch_shapes=[
             *[pltpu.VMEM((slots, 2, rows, quarter), BF16)] * OPS,
             pltpu.VMEM((ops, 2, XS - 1, 2, rows, quarter), BF16),
             pltpu.VMEM((ops, 2, rows, order), BF16),
             pltpu.VMEM((ops, 2, rows, order), BF16),
             pltpu.VMEM((2, order, order), BF16),
-            pltpu.VMEM((4 * rows, order), BF16),
-            pltpu.VMEM((4 * rows, order), BF16),
-            pltpu.VMEM((2, MODES, rows, 4 * rows), BF16),
-            pltpu.VMEM((2, MODES, rows, 4 * rows), BF16),
+            pltpu.VMEM((256, order), BF16),
+            pltpu.VMEM((256, order), BF16),
+            pltpu.VMEM((2 * rows, 2 * order), BF16),
+            pltpu.VMEM((ops, MODES, rows // 2, 4 * rows), BF16),
+            pltpu.VMEM((ops, MODES, rows // 2, 4 * rows), BF16),
             pltpu.VMEM((ops, 2, rows, order), BF16),
             pltpu.VMEM((XS, 8, 128), jnp.int32),
             pltpu.SMEM((XS, 8, 128), jnp.int32),
@@ -388,9 +409,9 @@
             dma((OPS,)), dma((OPS,)),
             dma((OPS, 2, XS - 1)), dma((OPS, 2, XS - 1)),
             dma((24,)), dma((24,)),
-            dma((2, MODES)), dma((2, MODES)),
+            dma((OPS, MODES)), dma((OPS, MODES)),
             dma((MODES,)), dma((MODES,)),
-            dma((2 + OPS + 2,)), dma((2,)),
+            dma((2 + OPS + OPS,)),
         ],
         compiler_params=pltpu.CompilerParams(
             collective_id=0, has_side_effects=True, vmem_limit_bytes=56 << 20

time: 119 us -> 113 us (0.950)
  Pallas kernels: 113 us -> 110 us
  local copies, waits for them, and re-layouts: 4.49 us -> 2 us
    pallas_call x1, Pallas kernels: 113 us -> 110 us  [body(): pl.pallas_call(kernel, out_shape=(pltpu.VMEM(elementals.shape, BF16), plt...]
    unnamed x2, local copies, waits for them, and re-layouts: 4.49 us -> 2 us
where the time goes in v4:
time: 113 us
  Pallas kernels  110 us (97%)
  local copies, waits for them, and re-layouts  2 us (2%)
    pallas_call x1, Pallas kernels, body(): pl.pallas_call(kernel, out_shape=(pltpu.VMEM(elementals.shape, BF16), plt...  110 us

profile of v4, /device:TPU:1, one launch (start us, length us, event | category | flops | bytes accessed | tf_op | source)
XLA Modules:
  0.0 113.1 jit_solution(16191586235283875338)
XLA Ops:
  0.6 110.4 %meson.1 = (bf16[1,4,2,96,1536]{4,3,2,1,0:T(8,128)(2,1)S(1)}, f32[1,4,2,4]{3,2,1,0:T(2,128)S(1)}) custom-call(s32[1,2]{1,0:T(1,128)} %times.1, s32[8]{0:T(128)} %slots.1, bf16[1,4,2,96,1536]{4,3,2,1,0:T(8,128)(2,1)} %elem_ref.1, bf16[1,2,96,1536]{3,2,1,0:T(8,128)(2,1)} %prop_ref.1), custom_call_target="tpu_custom_call" | custom-call | tf_op jit(solution)/shard_map/meson/pallas_call | solution.py:378
  111.1 0.6 copy.8
  111.6 1.4 %copy.9 = bf16[1,4,2,96,1536]{4,3,2,1,0:T(8,128)(2,1)} copy(bf16[1,4,2,96,1536]{4,3,2,1,0:T(8,128)(2,1)S(1)} %get-tuple-element.7) | data formatting | bytes 4718592

commit v5 on v4

--- a/solution.py
+++ b/solution.py
@@ -14,9 +14,9 @@
 SLOTS = 8
 
 
-def kernel(times, slots, elem_ref, prop_ref, sink_ref, corr_ref,
+def kernel(times_ref, slots_ref, elem_ref, prop_ref, sink_ref, corr_ref,
            r0, r1, r2, r3, staged, w_sink, w_source, tau, stack, stack2, left, turned, arrived, aligned,
-           want_all, want_smem, lines, parts,
+           times, slots, want_all, want_smem, lines, parts,
            want_send, want_recv, p1_send, p1_recv, y_send, y_recv, p2_send, p2_recv,
            tau_send, tau_recv, t_send, t_recv, ps_send, ps_recv, local):
     elem, prop, sink = elem_ref.at[0], prop_ref.at[0], sink_ref.at[0]
@@ -46,8 +46,10 @@
             src_ref=src, dst_ref=dst, send_sem=send, recv_sem=recv,
             device_id=device, device_id_type=MESH)
 
-    line = lax.broadcasted_iota(jnp.int32, (8, 128), 0)
-    want_all[x] = jnp.where(line == 0, slots[times[0, 0]], slots[times[0, 1]])
+    load_times = pltpu.make_async_copy(times_ref, times, local.at[0])
+    load_slots = pltpu.make_async_copy(slots_ref, slots, local.at[2 + 2 * OPS])
+    load_times.start()
+    load_slots.start()
 
     barrier = pltpu.get_barrier_semaphore()
     for step in range(1, XS):
@@ -59,13 +61,6 @@
         pl.semaphore_signal(barrier, inc=1, device_id=(pair, (mode + step) % MODES), device_id_type=MESH)
 
     pl.semaphore_wait(barrier, XS - 1 + 1 + MODES - 1)
-
-    want_copies = [
-        remote(want_all.at[x], want_all.at[x], want_send.at[s - 1], want_recv.at[s - 1], at_x(s))
-        for s in range(1, XS)
-    ]
-    for copy in want_copies:
-        copy.start()
 
     def columns(at):
         return pl.ds(pl.multiple_of(at * quarter, 128), quarter)
@@ -101,16 +96,30 @@
     up, down, sibling = at_mode(yl, zp, core), at_mode(yl, zm, core), at_mode(yl, z, 1 - core)
     own_chunk = chunk(yl, z, core)
 
+    pass_on("y", prop, tau_rows(own_chunk), at_mode(1 - yl, z, core))
     for copy in first[0][0]:
         copy.start()
     first[0][1].start()
-    pass_on("y", prop, tau_rows(own_chunk), at_mode(1 - yl, z, core))
     pass_on("z+", prop, tau_rows(own_chunk), up)
     pass_on("z-", prop, tau_rows(own_chunk), down)
     pass_on("c", prop, tau_rows(own_chunk), sibling)
     own_tau = pltpu.make_async_copy(prop, tau_rows(own_chunk), local.at[1 + OPS])
     own_tau.start()
-    for o in range(1, OPS):
+    for copy in first[1][0]:
+        copy.start()
+    first[1][1].start()
+
+    load_times.wait()
+    load_slots.wait()
+    line = lax.broadcasted_iota(jnp.int32, (8, 128), 0)
+    want_all[x] = jnp.where(line == 0, slots[times[0, 0]], slots[times[0, 1]])
+    want_copies = [
+        remote(want_all.at[x], want_all.at[x], want_send.at[s - 1], want_recv.at[s - 1], at_x(s))
+        for s in range(1, XS)
+    ]
+    for copy in want_copies:
+        copy.start()
+    for o in range(2, OPS):
         for copy in first[o][0]:
             copy.start()
         first[o][1].start()
@@ -252,13 +261,12 @@
 
     tall = 16
 
-    def align(o):
+    def align(o, then=None, start=()):
         group = lax.broadcasted_iota(jnp.int32, (tall, span), 1) // rows
         picks = [group == b for b in range(3)]
         own_slab(o).wait()
 
-        @pl.loop(0, MODES // 4)
-        def _(step):
+        def from_group(step, sums):
             g = (mode // 4 + step) % 4
 
             @pl.loop(4 * g, 4 * g + 4)
@@ -281,13 +289,16 @@
                     down_to = pl.ds(pl.multiple_of((a // 2) * half + it * tall, tall), tall)
                     aligned[o, a % 2, down_to, pl.ds(pl.multiple_of(g * span, 128), span)] = part.astype(BF16)
 
-    part_wide = 256
-
-    def contract(os, qs):
+            return sums if then is None else then(g, sums)
+
+        return lax.fori_loop(0, MODES // 4, from_group, start)
+
+    def terms(os, qs, at, sums):
+        wide = at.size
+
         def body(it, sums):
             sums = list(sums)
-            row = pl.ds(pl.multiple_of((it // 6) * tall, tall), tall)
-            at = pl.ds(pl.multiple_of((it % 6) * part_wide, 128), part_wide)
+            row = pl.ds(pl.multiple_of(it * tall, tall), tall)
             right = [(aligned[q, 0, row, at].astype(F32), aligned[q, 1, row, at].astype(F32)) for q in qs]
             k = 0
             for o in os:
@@ -295,12 +306,17 @@
                 for t_re, t_im in right:
                     for value in (s_re * t_re + s_im * t_im, s_im * t_re - s_re * t_im):
                         value = value[:8] + value[8:]
-                        sums[k] += value[:, :128] + value[:, 128:]
+                        for lanes in range(0, wide, 128):
+                            sums[k] += value[:, lanes:lanes + 128]
                         k += 1
             return tuple(sums)
 
-        zero = jnp.zeros((8, 128), F32)
-        sums = lax.fori_loop(0, (rows // tall) * (order // part_wide), body, (zero,) * (2 * len(os) * len(qs)))
+        return lax.fori_loop(0, rows // tall, body, sums)
+
+    def blank_sums(os, qs):
+        return (jnp.zeros((8, 128), F32),) * (2 * len(os) * len(qs))
+
+    def keep(os, qs, sums):
         k = 0
         for o in os:
             for q in qs:
@@ -308,6 +324,18 @@
                     index = q * 2 * OPS + 2 * o + part
                     lines[index:index + 1, :] = jnp.sum(sums[k], axis=0, keepdims=True)
                     k += 1
+
+    def contract(os, qs):
+        def body(it, sums):
+            return terms(os, qs, pl.ds(pl.multiple_of(it * 256, 128), 256), sums)
+
+        keep(os, qs, lax.fori_loop(0, order // 256, body, blank_sums(os, qs)))
+
+    def align_and_contract(o, os):
+        def then(g, sums):
+            return terms(os, (o,), pl.ds(pl.multiple_of(g * span, 128), span), sums)
+
+        keep(os, (o,), align(o, then, blank_sums(os, (o,))))
 
     source(0)
     sink_product(0)
@@ -324,8 +352,7 @@
     align(2)
     contract((3,), (0, 1))
     contract((0, 1, 2, 3), (2,))
-    align(3)
-    contract((0, 1, 2, 3), (3,))
+    align_and_contract(3, (0, 1, 2, 3))
 
     column = jnp.sum(lines[...], axis=1, keepdims=True)
     lane = lax.broadcasted_iota(jnp.int32, (2 * OPS, 128), 1)
@@ -382,8 +409,8 @@
             pltpu.VMEM((1, ops, 2, ops), F32),
         ),
         in_specs=[
-            pl.BlockSpec(memory_space=pltpu.SMEM),
-            pl.BlockSpec(memory_space=pltpu.SMEM),
+            pl.BlockSpec(memory_space=pl.ANY),
+            pl.BlockSpec(memory_space=pl.ANY),
             pl.BlockSpec(memory_space=pl.ANY),
             pl.BlockSpec(memory_space=pl.ANY),
         ],
@@ -400,6 +427,8 @@
             pltpu.VMEM((ops, MODES, rows // 2, 4 * rows), BF16),
             pltpu.VMEM((ops, MODES, rows // 2, 4 * rows), BF16),
             pltpu.VMEM((ops, 2, rows, order), BF16),
+            pltpu.SMEM(time_pairs.shape, jnp.int32),
+            pltpu.SMEM(slot_of.shape, jnp.int32),
             pltpu.VMEM((XS, 8, 128), jnp.int32),
             pltpu.SMEM((XS, 8, 128), jnp.int32),
             pltpu.VMEM((ops * ops * 2, 128), F32),
@@ -411,7 +440,7 @@
             dma((24,)), dma((24,)),
             dma((OPS, MODES)), dma((OPS, MODES)),
             dma((MODES,)), dma((MODES,)),
-            dma((2 + OPS + OPS,)),
+            dma((3 + OPS + OPS,)),
         ],
         compiler_params=pltpu.CompilerParams(
             collective_id=0, has_side_effects=True, vmem_limit_bytes=56 << 20

time: 113 us -> 112 us (level)
    pallas_call x1, Pallas kernels: 110 us -> 109 us  [body(): pl.pallas_call(kernel, out_shape=(pltpu.VMEM(elementals.shape, BF16), plt...]
where the time goes in v5:
time: 112 us
  Pallas kernels  109 us (97%)
  local copies, waits for them, and re-layouts  2 us (2%)
    pallas_call x1, Pallas kernels, body(): pl.pallas_call(kernel, out_shape=(pltpu.VMEM(elementals.shape, BF16), plt...  109 us

profile of v5, /device:TPU:1, one launch (start us, length us, event | category | flops | bytes accessed | tf_op | source)
XLA Modules:
  0.0 111.5 jit_solution(8856639353035848881)
XLA Ops:
  0.6 108.9 %meson.1 = (bf16[1,4,2,96,1536]{4,3,2,1,0:T(8,128)(2,1)S(1)}, f32[1,4,2,4]{3,2,1,0:T(2,128)S(1)}) custom-call(s32[1,2]{1,0:T(1,128)} %times_ref.1, s32[8]{0:T(128)} %slots_ref.1, bf16[1,4,2,96,1536]{4,3,2,1,0:T(8,128)(2,1)} %elem_ref.1, bf16[1,2,96,1536]{3,2,1,0:T(8,128)(2,1)} %prop_ref.1), custom_call_target="tpu_custom_call" | custom-call | tf_op jit(solution)/shard_map/meson/pallas_call | solution.py:405
  109.5 0.6 copy.8
  110.1 1.4 %copy.9 = bf16[1,4,2,96,1536]{4,3,2,1,0:T(8,128)(2,1)} copy(bf16[1,4,2,96,1536]{4,3,2,1,0:T(8,128)(2,1)S(1)} %get-tuple-element.7) | data formatting | bytes 4718592

commit v6 on v5

--- a/solution.py
+++ b/solution.py
@@ -218,12 +218,13 @@
         stack2[pl.ds(0, rows), :] = imag
         stack2[pl.ds(rows, rows), :] = real
 
-        blocks = 2 if o == OPS - 1 else 1
+        blocks = 2
         many = order // blocks
         owners = MODES // blocks
 
         @pl.loop(0, blocks)
-        def _(i):
+        def _(count):
+            i = (1 - yl + count) % 2
             at = pl.ds(pl.multiple_of(i * many, 16), many)
             total = lax.dot_general(tau[0, at, :], stack[...], dims, preferred_element_type=F32)
             total += lax.dot_general(tau[1, at, :], stack2[...], dims, preferred_element_type=F32)
@@ -342,15 +343,14 @@
     source(1)
     stage3(3)
     sink_product(1)
+    source(2)
     align(0)
-    source(2)
     sink_product(2)
     source(3)
     align(1)
-    contract((0, 1, 2), (0, 1))
     sink_product(3)
+    contract((0, 1, 2, 3), (0, 1))
     align(2)
-    contract((3,), (0, 1))
     contract((0, 1, 2, 3), (2,))
     align_and_contract(3, (0, 1, 2, 3))
 

time: 112 us -> 110 us (0.982)
  Pallas kernels: 109 us -> 107 us
    pallas_call x1, Pallas kernels: 109 us -> 107 us  [body(): pl.pallas_call(kernel, out_shape=(pltpu.VMEM(elementals.shape, BF16), plt...]
where the time goes in v6:
time: 110 us
  Pallas kernels  107 us (97%)
  local copies, waits for them, and re-layouts  2 us (2%)
    pallas_call x1, Pallas kernels, body(): pl.pallas_call(kernel, out_shape=(pltpu.VMEM(elementals.shape, BF16), plt...  107 us

profile of v6, /device:TPU:1, one launch (start us, length us, event | category | flops | bytes accessed | tf_op | source)
XLA Modules:
  0.0 109.5 jit_solution(14348962522596638952)
XLA Ops:
  0.6 106.9 %meson.1 = (bf16[1,4,2,96,1536]{4,3,2,1,0:T(8,128)(2,1)S(1)}, f32[1,4,2,4]{3,2,1,0:T(2,128)S(1)}) custom-call(s32[1,2]{1,0:T(1,128)} %times_ref.1, s32[8]{0:T(128)} %slots_ref.1, bf16[1,4,2,96,1536]{4,3,2,1,0:T(8,128)(2,1)} %elem_ref.1, bf16[1,2,96,1536]{3,2,1,0:T(8,128)(2,1)} %prop_ref.1), custom_call_target="tpu_custom_call" | custom-call | tf_op jit(solution)/shard_map/meson/pallas_call | solution.py:405
  107.5 0.6 copy.8
  108.1 1.4 %copy.9 = bf16[1,4,2,96,1536]{4,3,2,1,0:T(8,128)(2,1)} copy(bf16[1,4,2,96,1536]{4,3,2,1,0:T(8,128)(2,1)S(1)} %get-tuple-element.7) | data formatting | bytes 4718592

commit v7 on v6

--- a/solution.py
+++ b/solution.py
@@ -352,31 +352,6 @@
     contract((0, 1, 2, 3), (0, 1))
     align(2)
     contract((0, 1, 2, 3), (2,))
-    align_and_contract(3, (0, 1, 2, 3))
-
-    column = jnp.sum(lines[...], axis=1, keepdims=True)
-    lane = lax.broadcasted_iota(jnp.int32, (2 * OPS, 128), 1)
-    tile = jnp.zeros((2 * OPS, 128), F32)
-    for q in range(OPS):
-        tile = jnp.where(lane == q, column[2 * OPS * q:2 * OPS * (q + 1)], tile)
-    parts[mode] = tile
-
-    @pl.loop(1, MODES)
-    def _(step):
-        remote(parts.at[mode], parts.at[mode], ps_send.at[step], ps_recv.at[step],
-               (pair, (mode + step) % MODES)).start()
-
-    @pl.loop(1, MODES)
-    def _(step):
-        remote(parts.at[mode], parts.at[mode], ps_send.at[step], ps_recv.at[step],
-               (pair, (mode + step) % MODES)).wait()
-
-    total = parts[0]
-    for n in range(1, MODES):
-        total = total + parts[n]
-    total = total * (1.0 / order)
-    for o in range(OPS):
-        corr_ref[0, o] = total[2 * o:2 * o + 2, :OPS]
 
     for copy in want_copies:
         copy.wait_send()
@@ -389,12 +364,44 @@
         copy.wait_send()
     for copy in tau_copies.values():
         copy.wait_send()
-    for o in range(OPS):
+
+    def slabs_left(o):
         @pl.loop(0, MODES)
         def _(to):
             @pl.when(to != mode)
             def _():
                 slab(o, to, mode).wait_send()
+
+    slabs_left(0)
+    slabs_left(1)
+    align_and_contract(3, (0, 1, 2, 3))
+
+    column = jnp.sum(lines[...], axis=1, keepdims=True)
+    lane = lax.broadcasted_iota(jnp.int32, (2 * OPS, 128), 1)
+    tile = jnp.zeros((2 * OPS, 128), F32)
+    for q in range(OPS):
+        tile = jnp.where(lane == q, column[2 * OPS * q:2 * OPS * (q + 1)], tile)
+    parts[mode] = tile
+
+    @pl.loop(1, MODES)
+    def _(step):
+        remote(parts.at[mode], parts.at[mode], ps_send.at[step], ps_recv.at[step],
+               (pair, (mode + step) % MODES)).start()
+
+    slabs_left(2)
+    slabs_left(3)
+
+    @pl.loop(1, MODES)
+    def _(step):
+        remote(parts.at[mode], parts.at[mode], ps_send.at[step], ps_recv.at[step],
+               (pair, (mode + step) % MODES)).wait()
+
+    total = parts[0]
+    for n in range(1, MODES):
+        total = total + parts[n]
+    total = total * (1.0 / order)
+    for o in range(OPS):
+        corr_ref[0, o] = total[2 * o:2 * o + 2, :OPS]
 
 
 def body(time_pairs, slot_of, elementals, propagators):

time: 110 us -> 109 us (level)
  no operation moved by 1% of the time
where the time goes in v7:
time: 109 us
  Pallas kernels  106 us (97%)
  local copies, waits for them, and re-layouts  2 us (2%)
    pallas_call x1, Pallas kernels, body(): pl.pallas_call(kernel, out_shape=(pltpu.VMEM(elementals.shape, BF16), plt...  106 us

profile of v7, /device:TPU:1, one launch (start us, length us, event | category | flops | bytes accessed | tf_op | source)
XLA Modules:
  0.0 109.0 jit_solution(16620517256117182700)
XLA Ops:
  0.6 106.4 %meson.1 = (bf16[1,4,2,96,1536]{4,3,2,1,0:T(8,128)(2,1)S(1)}, f32[1,4,2,4]{3,2,1,0:T(2,128)S(1)}) custom-call(s32[1,2]{1,0:T(1,128)} %times_ref.1, s32[8]{0:T(128)} %slots_ref.1, bf16[1,4,2,96,1536]{4,3,2,1,0:T(8,128)(2,1)} %elem_ref.1, bf16[1,2,96,1536]{3,2,1,0:T(8,128)(2,1)} %prop_ref.1), custom_call_target="tpu_custom_call" | custom-call | tf_op jit(solution)/shard_map/meson/pallas_call | solution.py:412
  107.0 0.6 copy.8
  107.6 1.4 %copy.9 = bf16[1,4,2,96,1536]{4,3,2,1,0:T(8,128)(2,1)} copy(bf16[1,4,2,96,1536]{4,3,2,1,0:T(8,128)(2,1)S(1)} %get-tuple-element.7) | data formatting | bytes 4718592

commit v8 on v7

--- a/solution.py
+++ b/solution.py
@@ -119,10 +119,6 @@
     ]
     for copy in want_copies:
         copy.start()
-    for o in range(2, OPS):
-        for copy in first[o][0]:
-            copy.start()
-        first[o][1].start()
 
     plane = pl.ds(yh * XS, XS)
     across = [
@@ -136,6 +132,10 @@
         for copy in copies:
             copy.wait_recv()
         across[o].start()
+        if o + 2 < OPS:
+            for copy in first[o + 2][0]:
+                copy.start()
+            first[o + 2][1].start()
 
     second = {}
 

time: 109 us -> 109 us (level)
  no operation moved by 1% of the time
where the time goes in v8:
time: 109 us
  Pallas kernels  106 us (97%)
  local copies, waits for them, and re-layouts  2 us (2%)
    pallas_call x1, Pallas kernels, body(): pl.pallas_call(kernel, out_shape=(pltpu.VMEM(elementals.shape, BF16), plt...  106 us

profile of v8, /device:TPU:1, one launch (start us, length us, event | category | flops | bytes accessed | tf_op | source)
XLA Modules:
  0.0 109.0 jit_solution(6142011519183796212)
XLA Ops:
  0.6 106.4 %meson.1 = (bf16[1,4,2,96,1536]{4,3,2,1,0:T(8,128)(2,1)S(1)}, f32[1,4,2,4]{3,2,1,0:T(2,128)S(1)}) custom-call(s32[1,2]{1,0:T(1,128)} %times_ref.1, s32[8]{0:T(128)} %slots_ref.1, bf16[1,4,2,96,1536]{4,3,2,1,0:T(8,128)(2,1)} %elem_ref.1, bf16[1,2,96,1536]{3,2,1,0:T(8,128)(2,1)} %prop_ref.1), custom_call_target="tpu_custom_call" | custom-call | tf_op jit(solution)/shard_map/meson/pallas_call | solution.py:412
  107.0 0.6 copy.8
  107.6 1.4 %copy.9 = bf16[1,4,2,96,1536]{4,3,2,1,0:T(8,128)(2,1)} copy(bf16[1,4,2,96,1536]{4,3,2,1,0:T(8,128)(2,1)S(1)} %get-tuple-element.7) | data formatting | bytes 4718592
